TPU v7x, 128 devices: a whole 4x4x4 slice. The times are simulated.
128 devices in a mesh: train: 8 (over z_hi, y), query: 16 (over z_lo, x, core).
Axes of the slice: x: 4, y: 4, z: 4 (z_hi: 2, z_lo: 2; z = z_hi * 2 + z_lo), core: 2. Of those that a mesh axis runs over, the one named last changes fastest.
Arguments:
- query_grads: bfloat16 [1024, 4096], P('query'), may hold values from -6 to 6
- precond: float32 [32, 128, 128], replicated, may hold values from -0.5 to 0.5
- train_grads: bfloat16 [262144, 4096], P(('train', 'query')), may hold values from -0.09375 to 0.09375
- query_owner: int32 [1024], replicated, may hold values from 0 to 1023, each once
Outputs:
- scores: bfloat16 [1024, 262144], P('query', 'train')
Inputs may be any that keep to these rules, and one draw needn't show every extreme that they name: `query_owner`: a permutation: every output row is the row of exactly one query.
All inputs are finite; a program needn't handle non-finite values.
Results may differ from a plain program's by a relative error of at most 0.0049.
Values may be sent and summed in bfloat16 or wider, within the bound.
A program may use at most 128 MiB of HBM per device.

v0:
```python
import jax
import jax.numpy as jnp
from jax import lax
from jax.sharding import PartitionSpec as P

K = 4096
BLK = 128
NB = 32


def condition(rows, precond):
    count = rows.shape[0]
    split = rows.astype(jnp.float32).reshape(count, NB, BLK)
    result = jnp.einsum("nbk,bkl->nbl", split, precond, precision=lax.Precision.HIGHEST)
    return result.reshape(count, K).astype(jnp.bfloat16)


def per_device(query_grads, precond, train_grads, query_owner):
    inverse = jnp.argsort(query_owner)
    tile = lax.dot_general(
        lax.all_gather(condition(query_grads, precond), "query", axis=0, tiled=True),
        train_grads,
        (((1,), (1,)), ((), ())),
        preferred_element_type=jnp.float32,
    )
    ordered = jnp.take(tile.astype(jnp.bfloat16), inverse, axis=0)
    return lax.all_to_all(ordered, "query", split_axis=0, concat_axis=1, tiled=True)


def solution(mesh):
    placed = (P("query", None), P(), P(("train", "query"), None), P())
    return jax.shard_map(
        per_device, mesh=mesh, in_specs=placed, out_specs=P("query", "train"), check_vma=False
    )
```

profile of v0, /device:TPU:1, one launch (start us, length us, event | category | flops | bytes accessed | tf_op | source)
XLA Modules:
  0.0 168.4 jit_solution(12259154130061903294)
XLA Ops:
  6.5 0.0 copy-start
  6.5 0.0 copy-start.1
  6.5 0.0 all-gather.2.cloned.1.call-start
  6.5 1.6 copy-done
  8.1 2.2 %fusion = bf16[32,8,8,128]{3,2,1,0:T(8,128)(2,1)S(1)} fusion(f32[32,128,128]{2,1,0:T(8,128)S(1)} %copy-done, bf16[64,4096]{1,0:T(8,128)(2,1)} %param.4), kind=kOutput, calls=%fused_computation.4 | convolution fusion | flops 402915328 | bytes 3145728 | tf_op jit(solution)/shard_map/nbk,bkl->nbl/dot_general | solution.py:14
  10.3 0.9 copy.18
  11.2 0.0 all-gather.2.cloned.1.call-update
  11.2 0.0 copy-done.1
  11.2 4.4 %sort.17 = (s32[1024]{0:T(1024)}, s32[1024]{0:T(1024)S(1)}) sort(s32[1024]{0:T(1024)S(1)} %copy-done.1, s32[1024]{0:T(1024)S(1)} %iota.4), dimensions={0}, to_apply=%region_0.0 | sort | flops 10240 | bytes 16384 | tf_op jit(solution)/shard_map/jit(argsort)/sort | solution.py:19
  15.6 0.1 broadcast_in_dim.14
  15.7 51.5 %all-gather.2.cloned.1.call-done = bf16[1024,4096]{1,0:T(8,128)(2,1)} async-done(((bf16[64,4096]{1,0:T(8,128)(2,1)}), bf16[1024,4096]{1,0:T(8,128)(2,1)}) %all-gather.2.cloned.1.call-update) | async-done | bytes 8388624 | tf_op jit(solution)/shard_map/all_gather | solution.py:21
  67.2 23.8 %convolution_convert_fusion = bf16[1024,2048]{1,0:T(8,128)(2,1)} fusion(bf16[1024,4096]{1,0:T(8,128)(2,1)} %all-gather.2.cloned.1.call-done, bf16[2048,4096]{1,0:T(8,128)(2,1)} %param.6), kind=kOutput, calls=%fused_computation.2 | convolution fusion | flops 17181966336 | bytes 29360128 | tf_op jit(solution)/shard_map/dot_general | solution.py:20
  90.9 11.6 %gather_fusion = bf16[1024,2048]{1,0:T(8,128)(2,1)} fusion(bf16[1024,2048]{1,0:T(8,128)(2,1)} %convolution_convert_fusion, s32[1024]{0:T(1024)S(1)} %fusion.3), kind=kCustom, calls=%fused_computation | custom fusion | bytes 8392704 | tf_op jit(solution)/shard_map/jit(_take)/gather | solution.py:26
  102.5 2.6 %broadcast_select_fusion = bf16[16,64,2048]{2,1,0:T(8,128)(2,1)S(1)} fusion(bf16[16,64,2048]{2,1,0:T(8,128)(2,1)} %bitcast.20, pred[16,64]{1,0:T(8,128)(4,1)S(1)} %broadcast_in_dim.14), kind=kLoop, calls=%fused_computation.1 | loop fusion | flops 2097152 | bytes 8389632 | tf_op jit(solution)/shard_map/jit(_take)/select_n | solution.py:26
  105.1 54.1 %all_to_all.16 = bf16[16,64,2048]{2,1,0:T(8,128)(2,1)S(1)} all-to-all(bf16[16,64,2048]{2,1,0:T(8,128)(2,1)S(1)} %broadcast_select_fusion), channel_id=1, replica_groups=mesh['train'=8,'query'=16] {'query'}, dimensions={0} | all-to-all | bytes 8388608 | tf_op jit(solution)/shard_map/all_to_all | solution.py:27
  159.3 2.3 %copy.12 = bf16[16,8,8,2048]{3,2,0,1:T(8,128)(2,1)} copy(bf16[16,8,8,2048]{3,2,1,0:T(8,128)(2,1)S(1)} %bitcast.21) | data formatting | bytes 8388608 | tf_op jit(solution)/shard_map/all_to_all | solution.py:27
  (3 shorter events, 0.0 us)
Async XLA Ops:
  6.5 1.6 copy-start
  6.5 4.7 %copy-start.1 = (s32[1024]{0:T(1024)S(1)}, s32[1024]{0:T(1024)}, u32[]{:S(2)}) copy-start(s32[1024]{0:T(1024)} %param.7) | copy-start | bytes 12292
  6.5 60.6 %all-gather.2.cloned.1.call-start = ((), (), s32[]{:S(2)}) async-start(), calls=%async_computation.1 | async-start | bytes 8912896 | tf_op jit(solution)/shard_map/all_gather | solution.py:21
Sparse Core Ops, SparseCore 0:
  11.3 55.7 all-gather.1
where the time goes:
time: 169 us; the launch traced here: 168 us
  blocking collectives  54.1 us (32%)
  waiting for transfers between devices  51.5 us (30%)
  matrix products  25.9 us (15%)
  local copies, waits for them, and re-layouts  16.4 us (10%)
  between operations  13.4 us (8%)
  other arithmetic  7.01 us (4%)
    all_to_all x1, blocking collectives, per_device(): lax.all_to_all(ordered, 'query', split_axis=0, concat_axis=1, tiled=True)  54.1 us
    all_gather x1, waiting for transfers between devices, per_device(): lax.all_gather(condition(query_grads, precond), 'query', axis=0, tiled=True)  51.5 us
    dot_general x1, matrix products, per_device(): lax.dot_general(lax.all_gather(condition(query_grads, precond), 'query',...  23.8 us
    gather x1, local copies, waits for them, and re-layouts, per_device(): ordered = jnp.take(tile.astype(jnp.bfloat16), inverse, axis=0)  11.6 us
    sort x1, other arithmetic, per_device(): inverse = jnp.argsort(query_owner)  4.36 us
  transfers between devices with their start and end apart: 1, of which 1 were waited for; matrix products, arithmetic and copies ran while one was open for 3% of the time, Pallas kernels for 0%

commit v1 on v0

v1 whole, which is shorter than its diff:
```python
import jax
import jax.numpy as jnp
from jax import lax
from jax.experimental import pallas as pl
from jax.experimental.pallas import tpu as pltpu
from jax.sharding import PartitionSpec as P

K = 4096
BLK = 128
QUERIES = 1024
OWN = 64
LOCAL = 2048
SLICE = 512
PART = 256
GROUP = 256
GROUPS = QUERIES // GROUP
BLOCKS = GROUP // OWN
CHUNK = 512
CHUNKS = LOCAL // CHUNK
MESH = pl.DeviceIdType.MESH


def kernel(qg, pc, tr, owner, out, qv, pv, ov, cond, src, hot, gath, train, tile,
           lsem, tsem, s1s, s1r, a_s, a_r, b_s, b_r, o_s, o_r, self_sem):
    t = lax.axis_index("train")
    q = lax.axis_index("query")
    zh, y = t // 4, t % 4
    zl, x, c = q // 8, (q // 2) % 4, q % 2

    over = ((1 - zh) * 4 + y, (1 - zl) * 8 + x * 2 + c)
    up = (zh * 4 + (y + 1) % 4, q)
    down = (zh * 4 + (y + 3) % 4, q)
    mate = (t, q + 1 - 2 * c)

    def chip(dx, z):
        return z * 8 + ((x + dx) % 4) * 2

    def block_owner(g, j):
        m, b = g // 2, g % 2
        first = j // 2 == 0
        z0 = m * b
        if isinstance(j, int):
            dx = (1 - m) * (1 + 2 * b) + 2 * m if first else (1 - m) * (3 - 2 * b)
            z = z0 if first else 1 - z0
        return chip(dx, z) + j % 2

    load_q = pltpu.make_async_copy(qg.at[:, pl.ds(pl.multiple_of(t * SLICE, SLICE), SLICE)], qv, lsem.at[0])
    load_p = pltpu.make_async_copy(pc.at[pl.ds(t * 4, 4)], pv, lsem.at[1])
    load_o = pltpu.make_async_copy(owner, ov, lsem.at[2])
    load_q.start()
    load_p.start()
    load_o.start()

    def load_t(n):
        rows = pl.ds(pl.multiple_of(n * CHUNK, CHUNK), CHUNK)
        return pltpu.make_async_copy(tr.at[rows], train.at[rows], tsem.at[n])

    for n in range(CHUNKS):
        load_t(n).start()

    barrier = pltpu.get_barrier_semaphore()
    others = [(t, (q + d) % 16) for d in range(1, 16)]
    for device in others + [over, up, down]:
        pl.semaphore_signal(barrier, inc=1, device_id=device, device_id_type=MESH)

    load_q.wait()
    load_p.wait()
    for k in range(4):
        rows = qv[:, k * BLK:(k + 1) * BLK].astype(jnp.float32)
        done = jnp.dot(rows, pv[k], precision=lax.Precision.HIGHEST, preferred_element_type=jnp.float32)
        cond[k // 2, :, (k % 2) * BLK:(k % 2 + 1) * BLK] = done.astype(jnp.bfloat16)
    mine = pl.ds(pl.multiple_of(q * OWN, OWN), OWN)
    src[mine, :] = cond[c]

    pl.semaphore_wait(barrier, 18)

    def to_query(i, dest):
        return pltpu.make_async_remote_copy(
            src_ref=cond.at[dest % 2], dst_ref=src.at[mine], send_sem=s1s.at[i], recv_sem=s1r.at[q],
            device_id=(t, dest), device_id_type=MESH)

    dests = []
    for g in range(GROUPS):
        for j in range(BLOCKS):
            dests.append(block_owner(g, j))
    for i, dest in enumerate(dests):
        @pl.when(dest != q)
        def _():
            to_query(i, dest).start()

    load_o.wait()
    names = ov[...]
    for i, dest in enumerate(dests):
        row = lax.broadcasted_iota(jnp.int32, (OWN, QUERIES), 0) + dest * OWN
        hot[i * OWN:(i + 1) * OWN, :] = jnp.where(row == names, 1.0, 0.0).astype(jnp.bfloat16)

    for d in range(1, 16):
        frm = (q + d) % 16
        pltpu.make_async_remote_copy(
            src_ref=cond.at[0], dst_ref=src.at[pl.ds(pl.multiple_of(frm * OWN, OWN), OWN)],
            send_sem=s1s.at[0], recv_sem=s1r.at[frm], device_id=(t, frm), device_id_type=MESH).wait_recv()

    def piece(g, other, dy, core):
        h = zh + other * (1 - 2 * zh)
        column = (h * 4 + (y + dy) % 4) * SLICE + core * PART
        return gath.at[pl.ds(pl.multiple_of(g * GROUP, GROUP), GROUP), pl.ds(pl.multiple_of(column, PART), PART)]

    sent = ((0, 0, over), (0, 0, up), (0, 0, down), (1, 0, up), (1, 0, down), (0, 3, up), (1, 1, down))
    comes = ((1, 0), (0, 3), (0, 1), (1, 3), (1, 1), (0, 2), (1, 2))

    def link(g, i):
        other, dy, device = sent[i]
        part = piece(g, other, dy, c)
        return pltpu.make_async_remote_copy(
            src_ref=part, dst_ref=part, send_sem=a_s.at[g, i], recv_sem=a_r.at[g, i],
            device_id=device, device_id_type=MESH)

    def arrived(g, i):
        part = piece(g, *comes[i], c)
        pltpu.make_async_remote_copy(
            src_ref=part, dst_ref=part, send_sem=a_s.at[g, i], recv_sem=a_r.at[g, i],
            device_id=mate, device_id_type=MESH).wait_recv()

    pieces = ((0, 0),) + comes

    def share(g, i):
        part = piece(g, *pieces[i], c)
        return pltpu.make_async_remote_copy(
            src_ref=part, dst_ref=part, send_sem=b_s.at[g, i], recv_sem=b_r.at[g, i],
            device_id=mate, device_id_type=MESH)

    def shared(g, i):
        part = piece(g, *pieces[i], 1 - c)
        pltpu.make_async_remote_copy(
            src_ref=part, dst_ref=part, send_sem=b_s.at[g, i], recv_sem=b_r.at[g, i],
            device_id=mate, device_id_type=MESH).wait_recv()

    def order(g):
        rows = pl.ds(pl.multiple_of(g * GROUP, GROUP), GROUP)
        picked = jnp.dot(hot[rows, :], src[...], preferred_element_type=jnp.float32)
        column = pl.multiple_of(t * SLICE + c * PART, PART)
        gath[rows, pl.ds(column, PART)] = picked.astype(jnp.bfloat16)

    def step_a(g):
        link(g, 0).start()
        link(g, 1).start()
        link(g, 2).start()
        share(g, 0).start()

    def step_b(g):
        arrived(g, 0)
        link(g, 3).start()
        link(g, 4).start()
        share(g, 1).start()

    def step_c(g):
        arrived(g, 1)
        link(g, 5).start()
        share(g, 2).start()
        arrived(g, 2)
        share(g, 3).start()

    def step_d(g):
        arrived(g, 4)
        link(g, 6).start()
        share(g, 5).start()
        arrived(g, 3)
        share(g, 4).start()

    def step_e(g):
        arrived(g, 5)
        share(g, 6).start()
        arrived(g, 6)
        share(g, 7).start()
        for i in range(8):
            shared(g, i)

    order(0)
    step_a(0)
    for g in range(1, GROUPS):
        order(g)
    step_b(0)
    step_c(0)
    step_d(0)
    step_e(0)

    def deliver(g, j, n):
        dest = block_owner(g, j)
        rows = pl.ds(pl.multiple_of(g * GROUP + j * OWN, OWN), OWN)
        part = tile.at[rows, pl.ds(pl.multiple_of(n * CHUNK, CHUNK), CHUNK)]
        place = out.at[:, pl.ds(pl.multiple_of(q * LOCAL + n * CHUNK, CHUNK), CHUNK)]

        @pl.when(dest != q)
        def _():
            pltpu.make_async_remote_copy(
                src_ref=part, dst_ref=place, send_sem=o_s.at[g * BLOCKS + j], recv_sem=o_r.at[q],
                device_id=(t, dest), device_id_type=MESH).start()

        @pl.when(dest == q)
        def _():
            pltpu.make_async_copy(part, place, self_sem).start()

    def step(s, _):
        g, n = s // CHUNKS, s % CHUNKS
        after = g + 1
        more = after < GROUPS
        for k, do in enumerate((step_a, step_b, step_c, step_d)):
            @pl.when(jnp.logical_and(more, n == k))
            def _():
                do(after)

        @pl.when(g == 0)
        def _():
            load_t(n).wait()
        rows = pl.ds(pl.multiple_of(g * GROUP, GROUP), GROUP)
        cols = pl.ds(pl.multiple_of(n * CHUNK, CHUNK), CHUNK)
        scores = lax.dot_general(gath[rows, :], train[cols, :], (((1,), (1,)), ((), ())),
                                 preferred_element_type=jnp.float32)
        tile[rows, cols] = scores.astype(jnp.bfloat16)
        for j in range(BLOCKS):
            deliver(g, j, n)

        @pl.when(jnp.logical_and(more, n == CHUNKS - 1))
        def _():
            step_e(after)
        return 0

    lax.fori_loop(0, GROUPS * CHUNKS, step, 0)

    for d in range(1, 16):
        frm = (q + d) % 16
        place = out.at[:, pl.ds(pl.multiple_of(frm * LOCAL, LOCAL), LOCAL)]
        pltpu.make_async_remote_copy(
            src_ref=place, dst_ref=place, send_sem=o_s.at[0], recv_sem=o_r.at[frm],
            device_id=(t, frm), device_id_type=MESH).wait_recv()
    for i, dest in enumerate(dests):
        block = tile.at[pl.ds(i * OWN, OWN)]

        @pl.when(dest != q)
        def _():
            to_query(i, dest).wait_send()
            pltpu.make_async_remote_copy(
                src_ref=block, dst_ref=block, send_sem=o_s.at[i], recv_sem=o_r.at[q],
                device_id=(t, dest), device_id_type=MESH).wait_send()

        @pl.when(dest == q)
        def _():
            pltpu.make_async_copy(block, out.at[:, pl.ds(pl.multiple_of(q * LOCAL, LOCAL), LOCAL)], self_sem).wait()
    for g in range(GROUPS):
        for i in range(7):
            link(g, i).wait_send()
        for i in range(8):
            share(g, i).wait_send()


def per_device(query_grads, precond, train_grads, query_owner):
    dma = pltpu.SemaphoreType.DMA
    return pl.pallas_call(
        kernel,
        out_shape=jax.ShapeDtypeStruct((OWN, 16 * LOCAL), jnp.bfloat16),
        in_specs=[pl.BlockSpec(memory_space=pl.ANY)] * 4,
        out_specs=pl.BlockSpec(memory_space=pl.ANY),
        scratch_shapes=[
            pltpu.VMEM((OWN, SLICE), jnp.bfloat16),
            pltpu.VMEM((4, BLK, BLK), jnp.float32),
            pltpu.VMEM((1, QUERIES), jnp.int32),
            pltpu.VMEM((2, OWN, PART), jnp.bfloat16),
            pltpu.VMEM((QUERIES, PART), jnp.bfloat16),
            pltpu.VMEM((QUERIES, QUERIES), jnp.bfloat16),
            pltpu.VMEM((QUERIES, K), jnp.bfloat16),
            pltpu.VMEM((LOCAL, K), jnp.bfloat16),
            pltpu.VMEM((QUERIES, LOCAL), jnp.bfloat16),
            dma((3,)), dma((CHUNKS,)), dma((16,)), dma((16,)),
            dma((GROUPS, 7)), dma((GROUPS, 7)), dma((GROUPS, 8)), dma((GROUPS, 8)),
            dma((16,)), dma((16,)), dma,
        ],
        compiler_params=pltpu.CompilerParams(
            collective_id=0, has_side_effects=True, vmem_limit_bytes=56 << 20),
        cost_estimate=pl.CostEstimate(
            flops=2 * QUERIES * LOCAL * K, bytes_accessed=24 << 20, transcendentals=0),
        name="influence",
    )(query_grads, precond, train_grads, query_owner.reshape(1, QUERIES))


def solution(mesh):
    placed = (P("query", None), P(), P(("train", "query"), None), P())
    return jax.shard_map(
        per_device, mesh=mesh, in_specs=placed, out_specs=P("query", "train"), check_vma=False
    )
```

time: 169 us -> 98.1 us (0.58)
  Pallas kernels: 0 us -> 93.5 us
  blocking collectives: 54.1 us -> 0 us
  waiting for transfers between devices: 51.5 us -> 0 us
  matrix products: 25.9 us -> 0 us
  between operations: 13.4 us -> 0.01 us
  local copies, waits for them, and re-layouts: 16.4 us -> 4.47 us
  other arithmetic: 7.01 us -> 0 us
    pallas_call x0 -> x1, Pallas kernels: none -> 93.5 us  [per_device(): pl.pallas_call(kernel, out_shape=jax.ShapeDtypeStruct((OWN, 16 * LOCAL),...]
    all_to_all x1 -> x0, blocking collectives: 54.1 us -> none  [per_device(): lax.all_to_all(ordered, 'query', split_axis=0, concat_axis=1, tiled=True)]
    all_gather x1 -> x0, waiting for transfers between devices: 51.5 us -> none  [per_device(): lax.all_gather(condition(query_grads, precond), 'query', axis=0, tiled=True)]
    dot_general x2 -> x0, matrix products: 25.9 us -> none  [the longest x1 23.8 us: per_device(): lax.dot_general(lax.all_gather(condition(query_grads, precond), 'query',...]
    gather x1 -> x0, local copies, waits for them, and re-layouts: 11.6 us -> none  [per_device(): ordered = jnp.take(tile.astype(jnp.bfloat16), inverse, axis=0)]
    sort x1 -> x0, other arithmetic: 4.36 us -> none  [per_device(): inverse = jnp.argsort(query_owner)]
    unnamed x4 -> x1, local copies, waits for them, and re-layouts: 1.59 us -> 4.47 us
    select_n x1 -> x0, other arithmetic: 2.63 us -> none  [per_device(): ordered = jnp.take(tile.astype(jnp.bfloat16), inverse, axis=0)]
  transfers between devices with their start and end apart: 1 -> 0, of which waited for: 1 -> 0; matrix products, arithmetic and copies ran while one was open for 3% -> 0% of each run, Pallas kernels for 0% -> 0%
where the time goes in v1:
time: 98.1 us; the launch traced here: 97.9 us
  Pallas kernels  93.5 us (95%)
  local copies, waits for them, and re-layouts  4.47 us (5%)
    pallas_call x1, Pallas kernels, per_device(): pl.pallas_call(kernel, out_shape=jax.ShapeDtypeStruct((OWN, 16 * LOCAL),...  93.5 us
    unnamed x1, local copies, waits for them, and re-layouts  4.47 us

profile of v1, /device:TPU:1, one launch (start us, length us, event | category | flops | bytes accessed | tf_op | source)
XLA Modules:
  0.0 97.9 jit_solution(113189725616392711)
XLA Ops:
  0.0 93.5 %influence.1 = bf16[64,32768]{1,0:T(8,128)(2,1)} custom-call(bf16[64,4096]{1,0:T(8,128)(2,1)} %qg.1, f32[32,128,128]{2,1,0:T(8,128)} %pc.1, bf16[2048,4096]{1,0:T(8,128)(2,1)} %tr.1, s32[1,1024]{1,0:T(1,128)} %bitcast.1), custom_call_target="tpu_custom_call" | custom-call | flops 17179869184 | bytes 25165824 | tf_op jit(solution)/shard_map/influence/pallas_call | solution.py:258
  93.5 4.5 %copy.6 = bf16[64,32768]{1,0:T(8,128)(2,1)} copy(bf16[64,32768]{1,0:T(8,128)(2,1)} %influence.1) | data formatting | bytes 8388608

commit v2 on v0

v2 whole, which is shorter than its diff:
```python
import jax
import jax.numpy as jnp
from jax import lax
from jax.experimental import pallas as pl
from jax.experimental.pallas import tpu as pltpu
from jax.sharding import PartitionSpec as P

K = 4096
BLK = 128
QUERIES = 1024
OWN = 64
LOCAL = 2048
SLICE = 512
PART = 256
UNIT = 128
UNITS = QUERIES // UNIT
BLOCKS = UNIT // OWN
SINGLE = 4
CHUNK = 512
CHUNKS = LOCAL // CHUNK
MESH = pl.DeviceIdType.MESH


def kernel(qg, pc, tr, owner, out, qv, pv, ov, cond, src, hot, gath, train, tile,
           lsem, tsem, s1s, s1r, d_s, d_r, e_s, e_r, a_s, a_r, b_s, b_r, o_s, o_r, self_sem):
    t = lax.axis_index("train")
    q = lax.axis_index("query")
    zh, y = t // 4, t % 4
    zl, x, c = q // 8, (q // 2) % 4, q % 2

    over = ((1 - zh) * 4 + y, (1 - zl) * 8 + x * 2 + c)
    up = (zh * 4 + (y + 1) % 4, q)
    down = (zh * 4 + (y + 3) % 4, q)
    mate = (t, q + 1 - 2 * c)

    def apart(other, dy):
        h = zh + other * (1 - 2 * zh)
        z = zl + other * (1 - 2 * zl)
        return (h * 4 + (y + dy) % 4, z * 8 + x * 2 + c)

    ways = ((0, 1), (0, 3), (0, 2), (1, 0), (1, 1), (1, 3), (1, 2))

    def chip(dx, z):
        return z * 8 + ((x + dx) % 4) * 2

    def block_owner(u, j):
        m, b = u // 4, (u // 2) % 2
        dx = (1 - m) * (1 + 2 * b) + 2 * m if j == 0 else (1 - m) * (3 - 2 * b)
        z = m * b if j == 0 else 1 - m * b
        return chip(dx, z) + u % 2

    load_q = pltpu.make_async_copy(qg.at[:, pl.ds(pl.multiple_of(t * SLICE, SLICE), SLICE)], qv, lsem.at[0])
    load_p = pltpu.make_async_copy(pc.at[pl.ds(t * 4, 4)], pv, lsem.at[1])
    load_o = pltpu.make_async_copy(owner, ov, lsem.at[2])
    load_q.start()
    load_p.start()
    load_o.start()

    def load_t(n):
        rows = pl.ds(pl.multiple_of(n * CHUNK, CHUNK), CHUNK)
        return pltpu.make_async_copy(tr.at[rows], train.at[rows], tsem.at[n])

    barrier = pltpu.get_barrier_semaphore()
    others = [(t, (q + d) % 16) for d in range(1, 16)]
    for device in others + [apart(*way) for way in ways[:4]]:
        pl.semaphore_signal(barrier, inc=1, device_id=device, device_id_type=MESH)

    load_q.wait()
    load_p.wait()
    for k in range(4):
        rows = qv[:, k * BLK:(k + 1) * BLK].astype(jnp.float32)
        done = jnp.dot(rows, pv[k], precision=lax.Precision.HIGHEST, preferred_element_type=jnp.float32)
        cond[k % 2, k // 2] = done.astype(jnp.bfloat16)
    mine = pl.ds(pl.multiple_of(q * OWN, OWN), OWN)
    for h in range(2):
        src[h, mine, :] = cond[h, c]
    for n in range(CHUNKS):
        load_t(n).start()

    pl.semaphore_wait(barrier, 19)

    def to_query(h, dest):
        return pltpu.make_async_remote_copy(
            src_ref=cond.at[h, dest % 2], dst_ref=src.at[h, mine], send_sem=s1s.at[h], recv_sem=s1r.at[h],
            device_id=(t, dest), device_id_type=MESH)

    def queries(h):
        part = src.at[h, pl.ds(0, 15 * OWN)]
        return pltpu.make_async_remote_copy(
            src_ref=part, dst_ref=part, send_sem=s1s.at[h], recv_sem=s1r.at[h],
            device_id=mate, device_id_type=MESH)

    dests = []
    for u in range(UNITS):
        for j in range(BLOCKS):
            dests.append(block_owner(u, j))
    for h in range(2):
        for i, dest in enumerate(dests):
            @pl.when(dest != q)
            def _():
                to_query(h, dest).start()

    load_o.wait()
    names = ov[...]
    for i, dest in enumerate(dests):
        row = lax.broadcasted_iota(jnp.int32, (OWN, QUERIES), 0) + dest * OWN
        hot[i * OWN:(i + 1) * OWN, :] = jnp.where(row == names, 1.0, 0.0).astype(jnp.bfloat16)

    def unit_rows(u):
        return pl.ds(pl.multiple_of(u * UNIT, UNIT), UNIT)

    def piece(u, other, dy, core):
        h = zh + other * (1 - 2 * zh)
        column = (h * 4 + (y + dy) % 4) * SLICE + core * PART
        return gath.at[unit_rows(u), pl.ds(pl.multiple_of(column, PART), PART)]

    sent = ((0, 0, over), (0, 0, up), (0, 0, down), (1, 0, up), (1, 0, down), (0, 3, up), (1, 1, down))
    comes = ((1, 0), (0, 3), (0, 1), (1, 3), (1, 1), (0, 2), (1, 2))

    def link(u, i):
        other, dy, device = sent[i]
        part = piece(u, other, dy, c)
        return pltpu.make_async_remote_copy(
            src_ref=part, dst_ref=part, send_sem=a_s, recv_sem=a_r.at[u - 1, (0, 1, 1, 1, 1, 2, 2)[i]],
            device_id=device, device_id_type=MESH)

    def arrived(u, k):
        part = gath.at[pl.ds(0, UNIT * (1, 4, 2)[k]), pl.ds(0, PART)]
        pltpu.make_async_remote_copy(
            src_ref=part, dst_ref=part, send_sem=a_s, recv_sem=a_r.at[u - 1, k],
            device_id=mate, device_id_type=MESH).wait_recv()

    pieces = ((0, 0),) + comes

    def share(u, i):
        part = piece(u, *pieces[i], c)
        return pltpu.make_async_remote_copy(
            src_ref=part, dst_ref=part, send_sem=b_s, recv_sem=b_r.at[u - 1],
            device_id=mate, device_id_type=MESH)

    def whole(u):
        part = gath.at[pl.ds(0, 8 * UNIT), pl.ds(0, PART)]
        pltpu.make_async_remote_copy(
            src_ref=part, dst_ref=part, send_sem=b_s, recv_sem=b_r.at[u - 1],
            device_id=mate, device_id_type=MESH).wait_recv()

    def order(u, h):
        picked = jnp.dot(hot[unit_rows(u), :], src[h], preferred_element_type=jnp.float32)
        column = pl.multiple_of(t * SLICE + c * PART + h * BLK, BLK)
        gath[unit_rows(u), pl.ds(column, BLK)] = picked.astype(jnp.bfloat16)

    def half(other, dy, core, h):
        z = zh + other * (1 - 2 * zh)
        column = (z * 4 + (y + dy) % 4) * SLICE + core * PART + h * BLK
        return gath.at[pl.ds(0, UNIT), pl.ds(pl.multiple_of(column, BLK), BLK)]

    def direct(h, i):
        other, dy = ways[i]
        part = half(0, 0, c, h) if i < 4 else half(1, 0, c, h)
        return pltpu.make_async_remote_copy(
            src_ref=part, dst_ref=part, send_sem=d_s.at[h], recv_sem=d_r.at[h, i],
            device_id=apart(other, dy) if i < 4 else apart(0, dy), device_id_type=MESH)

    def came(h, i):
        part = half(ways[i][0], 4 - ways[i][1], c, h)
        pltpu.make_async_remote_copy(
            src_ref=part, dst_ref=part, send_sem=d_s.at[h], recv_sem=d_r.at[h, i],
            device_id=mate, device_id_type=MESH).wait_recv()

    def half_share(h, i):
        part = half(0, 0, c, h) if i == 7 else half(ways[i][0], 4 - ways[i][1], c, h)
        return pltpu.make_async_remote_copy(
            src_ref=part, dst_ref=part, send_sem=e_s.at[h], recv_sem=e_r.at[h],
            device_id=mate, device_id_type=MESH)

    def all_halves(h, count):
        part = src.at[h, pl.ds(0, count * UNIT)]
        return pltpu.make_async_remote_copy(
            src_ref=part, dst_ref=part, send_sem=d_s.at[h] if count == 7 else e_s.at[h], recv_sem=e_r.at[h],
            device_id=mate, device_id_type=MESH)

    def first_out(h):
        queries(h).wait_recv()
        order(0, h)
        for i in (3, 0, 1, 2):
            direct(h, i).start()
        half_share(h, 7).start()

    def first_over(h):
        came(h, 3)
        for i in (4, 5, 6):
            direct(h, i).start()
        half_share(h, 3).start()

    def first_in(h):
        for i in (0, 1, 2, 4, 5, 6):
            came(h, i)
            half_share(h, i).start()

    def own_out(u):
        link(u, 1).start()
        link(u, 2).start()
        share(u, 0).start()

    def over_out(u):
        arrived(u, 0)
        link(u, 3).start()
        link(u, 4).start()
        share(u, 1).start()

    def relay(u):
        arrived(u, 1)
        link(u, 5).start()
        link(u, 6).start()
        for i in (2, 3, 4, 5):
            share(u, i).start()

    def last(u):
        arrived(u, 2)
        share(u, 6).start()
        share(u, 7).start()

    def begin(u):
        if u + 1 < UNITS:
            link(u + 1, 0).start()
        own_out(u)
        over_out(u)

    def order_all(u):
        for h in range(2):
            order(u, h)

    first_out(0)
    first_over(0)
    first_out(1)
    for u in (1, 2):
        order_all(u)
        link(u, 0).start()
    first_over(1)
    own_out(1)
    over_out(1)
    own_out(2)
    first_in(0)
    for u in range(3, UNITS):
        order_all(u)
        if u == 3:
            link(u, 0).start()
    first_in(1)
    over_out(2)
    for h in range(2):
        all_halves(h, 8).wait_recv()

    plan = {1: (None, 1, 3), 3: (1, 2, 4), 6: (2, 3, 5), 9: (3, 4, 6), 12: (4, 5, 7),
            15: (5, 6, None), 17: (6, 7, None), 19: (7, None, None)}

    def serve(s):
        for when, (ending, passing, starting) in plan.items():
            @pl.when(s == when)
            def _():
                if ending is not None:
                    last(ending)
                if passing is not None:
                    relay(passing)
                if starting is not None:
                    begin(starting)

    def deliver(u, j, n):
        dest = block_owner(u, j)
        rows = pl.ds(pl.multiple_of(u * UNIT + j * OWN, OWN), OWN)
        part = tile.at[rows, pl.ds(pl.multiple_of(n * CHUNK, CHUNK), CHUNK)]
        place = out.at[:, pl.ds(pl.multiple_of(q * LOCAL + n * CHUNK, CHUNK), CHUNK)]

        @pl.when(dest != q)
        def _():
            pltpu.make_async_remote_copy(
                src_ref=part, dst_ref=place, send_sem=o_s, recv_sem=o_r,
                device_id=(t, dest), device_id_type=MESH).start()

        @pl.when(dest == q)
        def _():
            pltpu.make_async_copy(part, place, self_sem).start()

    def chunk_cols(n):
        return pl.ds(pl.multiple_of(n * CHUNK, CHUNK), CHUNK)

    def single(s, _):
        u, n = s // CHUNKS, s % CHUNKS

        serve(s)

        @pl.when(u == 0)
        def _():
            load_t(n).wait()
        scores = lax.dot_general(train[chunk_cols(n), :], gath[unit_rows(u), :], (((1,), (1,)), ((), ())),
                                 preferred_element_type=jnp.float32)
        tile[unit_rows(u), chunk_cols(n)] = scores.T.astype(jnp.bfloat16)
        for j in range(BLOCKS):
            deliver(u, j, n)

        @pl.when(n == CHUNKS - 1)
        def _():
            whole(u + 1)
        return 0

    lax.fori_loop(0, SINGLE * CHUNKS, single, 0)
    whole(SINGLE + 1)

    def pair(s, _):
        m, n = s // CHUNKS, s % CHUNKS
        u = SINGLE + 2 * m

        serve(s + SINGLE * CHUNKS)
        rows = pl.ds(pl.multiple_of(u * UNIT, UNIT), 2 * UNIT)
        scores = lax.dot_general(gath[rows, :], train[chunk_cols(n), :], (((1,), (1,)), ((), ())),
                                 preferred_element_type=jnp.float32)
        tile[rows, chunk_cols(n)] = scores.astype(jnp.bfloat16)
        for k in range(2):
            for j in range(BLOCKS):
                deliver(u + k, j, n)

        @pl.when(s == CHUNKS - 1)
        def _():
            whole(SINGLE + 2)
            whole(SINGLE + 3)
        return 0

    lax.fori_loop(0, 2 * CHUNKS, pair, 0)

    def ended(part, sem):
        return pltpu.make_async_remote_copy(
            src_ref=part, dst_ref=part, send_sem=sem, recv_sem=o_r, device_id=mate, device_id_type=MESH)

    for h in range(2):
        queries(h).wait_send()
        all_halves(h, 7).wait_send()
        all_halves(h, 8).wait_send()
    ended(gath.at[pl.ds(0, 7 * 7 * 16), pl.ds(0, 8 * PART)], a_s).wait_send()
    ended(gath.at[pl.ds(0, 7 * UNIT), pl.ds(0, 8 * PART)], b_s).wait_send()
    here = out.at[:, pl.ds(pl.multiple_of(q * LOCAL, LOCAL), LOCAL)]
    pltpu.make_async_copy(tile.at[pl.ds(0, OWN)], here, self_sem).wait()
    blocks = ended(tile.at[pl.ds(0, 15 * OWN)], o_s)
    blocks.wait_recv()
    blocks.wait_send()


def per_device(query_grads, precond, train_grads, query_owner):
    dma = pltpu.SemaphoreType.DMA
    return pl.pallas_call(
        kernel,
        out_shape=pltpu.VMEM((OWN, 16 * LOCAL), jnp.bfloat16),
        in_specs=[pl.BlockSpec(memory_space=pl.ANY)] * 4,
        out_specs=pl.BlockSpec(memory_space=pl.ANY),
        scratch_shapes=[
            pltpu.VMEM((OWN, SLICE), jnp.bfloat16),
            pltpu.VMEM((4, BLK, BLK), jnp.float32),
            pltpu.VMEM((1, QUERIES), jnp.int32),
            pltpu.VMEM((2, 2, OWN, BLK), jnp.bfloat16),
            pltpu.VMEM((2, QUERIES, BLK), jnp.bfloat16),
            pltpu.VMEM((QUERIES, QUERIES), jnp.bfloat16),
            pltpu.VMEM((QUERIES, K), jnp.bfloat16),
            pltpu.VMEM((LOCAL, K), jnp.bfloat16),
            pltpu.VMEM((QUERIES, LOCAL), jnp.bfloat16),
            dma((3,)), dma((CHUNKS,)), dma((2,)), dma((2,)),
            dma((2,)), dma((2, 7)), dma((2,)), dma((2,)),
            dma, dma((UNITS - 1, 3)), dma, dma((UNITS - 1,)),
            dma, dma, dma,
        ],
        compiler_params=pltpu.CompilerParams(
            collective_id=0, has_side_effects=True, vmem_limit_bytes=56 << 20),
        cost_estimate=pl.CostEstimate(
            flops=2 * QUERIES * LOCAL * K, bytes_accessed=24 << 20, transcendentals=0),
        name="influence",
    )(query_grads, precond, train_grads, query_owner.reshape(1, QUERIES))


def solution(mesh):
    placed = (P("query", None), P(), P(("train", "query"), None), P())
    return jax.shard_map(
        per_device, mesh=mesh, in_specs=placed, out_specs=P("query", "train"), check_vma=False
    )
```

time: 169 us -> 80.1 us (0.47)
  Pallas kernels: 0 us -> 78 us
  blocking collectives: 54.1 us -> 0 us
  waiting for transfers between devices: 51.5 us -> 0 us
  matrix products: 25.9 us -> 0 us
  local copies, waits for them, and re-layouts: 16.4 us -> 2.02 us
  between operations: 13.4 us -> 0.01 us
  other arithmetic: 7.01 us -> 0 us
    pallas_call x0 -> x1, Pallas kernels: none -> 78 us  [per_device(): pl.pallas_call(kernel, out_shape=pltpu.VMEM((OWN, 16 * LOCAL), jnp.bfloat...]
    all_to_all x1 -> x0, blocking collectives: 54.1 us -> none  [per_device(): lax.all_to_all(ordered, 'query', split_axis=0, concat_axis=1, tiled=True)]
    all_gather x1 -> x0, waiting for transfers between devices: 51.5 us -> none  [per_device(): lax.all_gather(condition(query_grads, precond), 'query', axis=0, tiled=True)]
    dot_general x2 -> x0, matrix products: 25.9 us -> none  [the longest x1 23.8 us: per_device(): lax.dot_general(lax.all_gather(condition(query_grads, precond), 'query',...]
    gather x1 -> x0, local copies, waits for them, and re-layouts: 11.6 us -> none  [per_device(): ordered = jnp.take(tile.astype(jnp.bfloat16), inverse, axis=0)]
    sort x1 -> x0, other arithmetic: 4.36 us -> none  [per_device(): inverse = jnp.argsort(query_owner)]
    select_n x1 -> x0, other arithmetic: 2.63 us -> none  [per_device(): ordered = jnp.take(tile.astype(jnp.bfloat16), inverse, axis=0)]
    all_to_all x1 -> x0, local copies, waits for them, and re-layouts: 2.32 us -> none  [per_device(): lax.all_to_all(ordered, 'query', split_axis=0, concat_axis=1, tiled=True)]
  transfers between devices with their start and end apart: 1 -> 0, of which waited for: 1 -> 0; matrix products, arithmetic and copies ran while one was open for 3% -> 0% of each run, Pallas kernels for 0% -> 0%
where the time goes in v2:
time: 80.1 us; the launch traced here: 80 us
  Pallas kernels  78 us (97%)
  local copies, waits for them, and re-layouts  2.02 us (3%)
    pallas_call x1, Pallas kernels, per_device(): pl.pallas_call(kernel, out_shape=pltpu.VMEM((OWN, 16 * LOCAL), jnp.bfloat...  78 us
    unnamed x1, local copies, waits for them, and re-layouts  2.02 us

profile of v2, /device:TPU:1, one launch (start us, length us, event | category | flops | bytes accessed | tf_op | source)
XLA Modules:
  0.0 80.0 jit_solution(13533537494640593412)
XLA Ops:
  0.0 78.0 %influence.1 = bf16[64,32768]{1,0:T(8,128)(2,1)S(1)} custom-call(bf16[64,4096]{1,0:T(8,128)(2,1)} %qg.1, f32[32,128,128]{2,1,0:T(8,128)} %pc.1, bf16[2048,4096]{1,0:T(8,128)(2,1)} %tr.1, s32[1,1024]{1,0:T(1,128)} %bitcast.1), custom_call_target="tpu_custom_call" | custom-call | flops 17179869184 | bytes 25165824 | tf_op jit(solution)/shard_map/influence/pallas_call | solution.py:348
  78.0 2.0 %copy.6 = bf16[64,32768]{1,0:T(8,128)(2,1)} copy(bf16[64,32768]{1,0:T(8,128)(2,1)S(1)} %influence.1) | data formatting | bytes 8388608

commit v3 on v2

--- a/solution.py
+++ b/solution.py
@@ -95,7 +95,7 @@
         for j in range(BLOCKS):
             dests.append(block_owner(u, j))
     for h in range(2):
-        for i, dest in enumerate(dests):
+        for dest in dests[::-1]:
             @pl.when(dest != q)
             def _():
                 to_query(h, dest).start()

time: 80.1 us -> 80.2 us (level)
  no operation moved by 1% of the time
where the time goes in v3:
time: 80.2 us; the launch traced here: 80 us
  Pallas kernels  78 us (97%)
  local copies, waits for them, and re-layouts  2.02 us (3%)
    pallas_call x1, Pallas kernels, per_device(): pl.pallas_call(kernel, out_shape=pltpu.VMEM((OWN, 16 * LOCAL), jnp.bfloat...  78 us
    unnamed x1, local copies, waits for them, and re-layouts  2.02 us

profile of v3, /device:TPU:1, one launch (start us, length us, event | category | flops | bytes accessed | tf_op | source)
XLA Modules:
  0.0 80.0 jit_solution(197633613740975922)
XLA Ops:
  0.0 78.0 %influence.1 = bf16[64,32768]{1,0:T(8,128)(2,1)S(1)} custom-call(bf16[64,4096]{1,0:T(8,128)(2,1)} %qg.1, f32[32,128,128]{2,1,0:T(8,128)} %pc.1, bf16[2048,4096]{1,0:T(8,128)(2,1)} %tr.1, s32[1,1024]{1,0:T(1,128)} %bitcast.1), custom_call_target="tpu_custom_call" | custom-call | flops 17179869184 | bytes 25165824 | tf_op jit(solution)/shard_map/influence/pallas_call | solution.py:348
  78.0 2.0 %copy.6 = bf16[64,32768]{1,0:T(8,128)(2,1)} copy(bf16[64,32768]{1,0:T(8,128)(2,1)S(1)} %influence.1) | data formatting | bytes 8388608

commit v4 on v2

--- a/solution.py
+++ b/solution.py
@@ -250,19 +250,19 @@
     for h in range(2):
         all_halves(h, 8).wait_recv()
 
-    plan = {1: (None, 1, 3), 3: (1, 2, 4), 6: (2, 3, 5), 9: (3, 4, 6), 12: (4, 5, 7),
+    plan = {1: (None, 1, 3), 3: (None, 2, 4), 6: (2, 3, 5), 9: (3, 4, 6), 12: (4, 5, 7),
             15: (5, 6, None), 17: (6, 7, None), 19: (7, None, None)}
 
     def serve(s):
         for when, (ending, passing, starting) in plan.items():
             @pl.when(s == when)
             def _():
-                if ending is not None:
-                    last(ending)
                 if passing is not None:
                     relay(passing)
                 if starting is not None:
                     begin(starting)
+                if ending is not None:
+                    last(ending)
 
     def deliver(u, j, n):
         dest = block_owner(u, j)
@@ -296,6 +296,10 @@
         tile[unit_rows(u), chunk_cols(n)] = scores.T.astype(jnp.bfloat16)
         for j in range(BLOCKS):
             deliver(u, j, n)
+
+        @pl.when(s == CHUNKS - 1)
+        def _():
+            last(1)
 
         @pl.when(n == CHUNKS - 1)
         def _():

time: 80.1 us -> 81.2 us (1.014); the launches traced: 80 us -> 80.3 us
  no operation moved by 1% of the time
where the time goes in v4:
time: 81.2 us; the launch traced here: 80.3 us
  Pallas kernels  78.2 us (96%)
  local copies, waits for them, and re-layouts  2.02 us (2%)
    pallas_call x1, Pallas kernels, per_device(): pl.pallas_call(kernel, out_shape=pltpu.VMEM((OWN, 16 * LOCAL), jnp.bfloat...  78.2 us
    unnamed x1, local copies, waits for them, and re-layouts  2.02 us

profile of v4, /device:TPU:1, one launch (start us, length us, event | category | flops | bytes accessed | tf_op | source)
XLA Modules:
  0.0 80.3 jit_solution(4910333781695324304)
XLA Ops:
  0.0 78.2 %influence.1 = bf16[64,32768]{1,0:T(8,128)(2,1)S(1)} custom-call(bf16[64,4096]{1,0:T(8,128)(2,1)} %qg.1, f32[32,128,128]{2,1,0:T(8,128)} %pc.1, bf16[2048,4096]{1,0:T(8,128)(2,1)} %tr.1, s32[1,1024]{1,0:T(1,128)} %bitcast.1), custom_call_target="tpu_custom_call" | custom-call | flops 17179869184 | bytes 25165824 | tf_op jit(solution)/shard_map/influence/pallas_call | solution.py:352
  78.2 2.0 %copy.6 = bf16[64,32768]{1,0:T(8,128)(2,1)} copy(bf16[64,32768]{1,0:T(8,128)(2,1)S(1)} %influence.1) | data formatting | bytes 8388608
